TPU v7x, 32 devices: a whole 2x2x4 slice. The times are simulated.
32 devices in a mesh: seq: 16 (over z, y, x), head: 2 (over core).
Axes of the slice: x: 2, y: 2, z: 4, core: 2. Of those that a mesh axis runs over, the one named last changes fastest.
Arguments:
- ssm_input: bfloat16 [16384, 4096], P('seq', 'head'), may hold values from -125 to 125
- gate_input: bfloat16 [16384, 4096], P('seq', 'head'), may hold values from -8 to 8
- write_proj: bfloat16 [16384, 128], P('seq'), may hold values from -0.1875 to 0.1875
- read_proj: bfloat16 [16384, 128], P('seq'), may hold values from -0.5 to 0.5
- decay_codes: int32 [32, 16384], P('head', 'seq'), may hold values from 1 to 32768
- decay_rate: float32 [32], P('head'), may hold values from 0.8 to 6000
- skip_gain: float32 [32], P('head'), may hold values from 0.5 to 1.5
- norm_gain: float32 [4096], P('head'), may hold values from 0.5 to 1.5
Outputs:
- mamba_out: bfloat16 [16384, 4096], P('seq', 'head')
All inputs are finite; a program needn't handle non-finite values.
Results may differ from a plain program's by a relative error of at most 0.0054.
Values sent between devices are 32-bit elements; how exact they have to be, the bound alone decides.
A program may use at most 64 MiB of HBM per device.

v0:
```python
import jax
import jax.numpy as jnp
from jax import lax
from jax.sharding import PartitionSpec as P

HEADS = 32
HEAD_DIM = 128
GROUP = 256


def passed_along(block, axis, distance):
    devices = range(lax.axis_size(axis))
    route = [(i - distance, i) for i in devices if i - distance in devices]
    return lax.ppermute(block, axis, route)


def local(
    ssm_input, gate_input, write_proj, read_proj, decay_codes, decay_rate, skip_gain, norm_gain
):
    row_count, width = ssm_input.shape
    local_heads = decay_rate.shape[0]
    head_width = width // local_heads
    block_count = row_count // GROUP
    state_width = write_proj.shape[1]
    total_rows = row_count * lax.axis_size("seq")
    log_decay = -(decay_codes.astype(jnp.float32) * decay_rate[:, None]) / (8.0 * total_rows)
    cumulative = jnp.cumsum(log_decay.reshape(local_heads, block_count, GROUP), axis=2)
    x_blocks = ssm_input.reshape(block_count, GROUP, local_heads, head_width)
    write_blocks = write_proj.reshape(block_count, GROUP, state_width)
    read_blocks = read_proj.reshape(block_count, GROUP, state_width)
    positions = jnp.arange(GROUP, dtype=jnp.int32)
    causal = positions[:, None] >= positions[None, :]
    scores = jnp.einsum(
        "ktn,ksn->kts", read_blocks, write_blocks, preferred_element_type=jnp.float32
    )
    spread = cumulative[:, :, :, None] - cumulative[:, :, None, :]
    decay_mask = jnp.where(causal, jnp.exp(jnp.where(causal, spread, 0.0)), 0.0)
    mixing = (decay_mask * scores[None]).astype(jnp.bfloat16)
    inner_out = jnp.einsum("hkts,kshp->kthp", mixing, x_blocks, preferred_element_type=jnp.float32)
    block_end = cumulative[:, :, -1]
    tail = jnp.exp(block_end[:, :, None] - cumulative).transpose(1, 2, 0)
    weighted = (tail[:, :, :, None] * x_blocks.astype(jnp.float32)).astype(jnp.bfloat16)
    block_state = jnp.einsum(
        "kqn,kqhp->khnp", write_blocks, weighted, preferred_element_type=jnp.float32
    )
    block_decay = jnp.exp(block_end).T

    def advance(running, block_items):
        decay_part, state_part = block_items
        return (decay_part[:, None, None] * running + state_part, running)

    empty = jnp.zeros((local_heads, state_width, head_width), jnp.float32)
    summary, _ = lax.scan(advance, empty, (block_decay, block_state))
    device_decay = jnp.exp(jnp.sum(block_end, axis=1))

    def relay_turn(turn, pair):
        received = passed_along(pair[1], "seq", 1)
        return (received, device_decay[:, None, None] * received + summary)

    incoming, _ = lax.fori_loop(0, lax.axis_size("seq") - 1, relay_turn, (empty, summary))
    _, entering = lax.scan(advance, incoming, (block_decay, block_state))
    read_out = jnp.einsum(
        "ktn,khnp->kthp",
        read_blocks,
        entering.astype(jnp.bfloat16),
        preferred_element_type=jnp.float32,
    )
    carried = jnp.exp(cumulative).transpose(1, 2, 0)[:, :, :, None] * read_out
    ssm_out = inner_out + carried + skip_gain[None, None, :, None] * x_blocks.astype(jnp.float32)
    ssm_out = ssm_out.reshape(row_count, width)
    gated_out = ssm_out * jax.nn.silu(gate_input.astype(jnp.float32))
    row_power = lax.psum(jnp.sum(gated_out * gated_out, axis=1), "head") / (HEADS * HEAD_DIM)
    return (gated_out * lax.rsqrt(row_power[:, None] + 1e-05) * norm_gain[None, :]).astype(
        jnp.bfloat16
    )


def solution(mesh):
    placed = (
        P("seq", "head"),
        P("seq", "head"),
        P("seq", None),
        P("seq", None),
        P("head", "seq"),
        P("head"),
        P("head"),
        P("head"),
    )
    return jax.shard_map(
        local, mesh=mesh, in_specs=placed, out_specs=P("seq", "head"), check_vma=False
    )
```

profile of v0, /device:TPU:27, one launch (start us, length us, event | category | flops | bytes accessed | tf_op | source)
XLA Modules:
  0.0 455.6 jit_solution(9267145339343530914)
XLA Ops:
  1.1 2.3 reduce-window.6
  4.0 3.6 copy.45
  7.6 1.9 copy-done.3
  9.5 6.5 %fusion.19 = f32[4,16,128,128]{2,3,1,0:T(8,128)} fusion(bf16[4,256,128,1]{2,1,3,0:T(8,128)(2,1)S(1)} %bitcast.80, f32[4,256,16]{1,2,0:T(8,128)S(1)} %get-tuple-element.156, bf16[4,256,16,128]{3,2,1,0:T(8,128)(2,1)S(1)} %bitcast.77), kind=kOutput, calls=%fused_computation.33 | convolution fusion | flops 543162368 | bytes 8716288 | tf_op jit(solution)/shard_map/kqn,kqhp->khnp/dot_general | solution.py:43
  16.0 5.4 %copy.34 = f32[4,16,128,128]{3,2,1,0:T(8,128)} copy(f32[4,16,128,128]{2,3,1,0:T(8,128)} %fusion.19) | data formatting | bytes 8388608
  21.4 5.8 %while.37 = (s32[]{:T(128)}, f32[16,128,128]{2,1,0:T(8,128)S(1)}, f32[4,16]{1,0:T(4,128)S(1)}, f32[4,16,128,128]{3,2,1,0:T(8,128)}, s32[]{:T(128)}, /*index=5*/s32[]{:T(128)}) while((s32[]{:T(128)}, f32[16,128,128]{2,1,0:T(8,128)S(1)}, f32[4,16]{1,0:T(4,128)S(1)}, f32[4,16,128,128]{3,2,1,0:T(8,128)}, s32[]{:T(128)}, ...), condition=%wide.region_3.4_spmd.clone, body=%wide.region_2.3_spmd.clone.sunk | while | flops 786435 | bytes 3146007 | solution.py:53
  21.4 1.4 bitcast_add_fusion.5
  22.8 1.4 bitcast_add_fusion.5
  24.3 1.4 bitcast_add_fusion.5
  25.7 1.4 bitcast_add_fusion.5
  28.2 361.4 %while.35 = (s32[]{:T(128)}, f32[16,128,128]{2,1,0:T(8,128)}, f32[16,128,128]{2,1,0:T(8,128)}, f32[16]{0:T(128)S(1)}, f32[16,128,128]{2,1,0:T(8,128)S(1)}, /*index=5*/s32[]{:T(128)}) while((s32[]{:T(128)}, f32[16,128,128]{2,1,0:T(8,128)}, f32[16,128,128]{2,1,0:T(8,128)}, f32[16]{0:T(128)S(1)}, f32[16,128,128]{2,1,0:T(8,128)S(1)}, ...), condition=%wide.region_6.7_spmd, body=%wide.region_5.6_spmd.sunk | while | flops 524290 | bytes 11534537 | solution.py:60
  28.2 3.1 collective-permute-start
  31.4 23.0 %collective-permute-done = f32[16,128,128]{2,1,0:T(8,128)S(1)} collective-permute-done((f32[16,128,128]{2,1,0:T(8,128)}, f32[16,128,128]{2,1,0:T(8,128)S(1)}, u32[]{:S(2)}, u32[]{:S(2)}) %collective-permute-start) | collective-permute-done | bytes 1048608 | tf_op jit(solution)/shard_map/while/body/eval_jaxpr/ppermute | solution.py:14
  54.4 1.4 multiply_add_fusion.2
  55.7 4.0 collective-permute-start
  59.8 22.1 %collective-permute-done = f32[16,128,128]{2,1,0:T(8,128)S(1)} collective-permute-done((f32[16,128,128]{2,1,0:T(8,128)}, f32[16,128,128]{2,1,0:T(8,128)S(1)}, u32[]{:S(2)}, u32[]{:S(2)}) %collective-permute-start) | collective-permute-done | bytes 1048608 | tf_op jit(solution)/shard_map/while/body/eval_jaxpr/ppermute | solution.py:14
  81.8 1.4 multiply_add_fusion.2
  83.2 4.0 collective-permute-start
  87.2 22.0 %collective-permute-done = f32[16,128,128]{2,1,0:T(8,128)S(1)} collective-permute-done((f32[16,128,128]{2,1,0:T(8,128)}, f32[16,128,128]{2,1,0:T(8,128)S(1)}, u32[]{:S(2)}, u32[]{:S(2)}) %collective-permute-start) | collective-permute-done | bytes 1048608 | tf_op jit(solution)/shard_map/while/body/eval_jaxpr/ppermute | solution.py:14
  109.3 1.4 multiply_add_fusion.2
  110.6 3.1 collective-permute-start
  113.8 22.0 %collective-permute-done = f32[16,128,128]{2,1,0:T(8,128)S(1)} collective-permute-done((f32[16,128,128]{2,1,0:T(8,128)}, f32[16,128,128]{2,1,0:T(8,128)S(1)}, u32[]{:S(2)}, u32[]{:S(2)}) %collective-permute-start) | collective-permute-done | bytes 1048608 | tf_op jit(solution)/shard_map/while/body/eval_jaxpr/ppermute | solution.py:14
  135.8 1.4 multiply_add_fusion.2
  137.2 2.3 collective-permute-start
  139.4 22.0 %collective-permute-done = f32[16,128,128]{2,1,0:T(8,128)S(1)} collective-permute-done((f32[16,128,128]{2,1,0:T(8,128)}, f32[16,128,128]{2,1,0:T(8,128)S(1)}, u32[]{:S(2)}, u32[]{:S(2)}) %collective-permute-start) | collective-permute-done | bytes 1048608 | tf_op jit(solution)/shard_map/while/body/eval_jaxpr/ppermute | solution.py:14
  161.4 1.4 multiply_add_fusion.2
  162.8 1.9 collective-permute-start
  164.7 21.4 %collective-permute-done = f32[16,128,128]{2,1,0:T(8,128)S(1)} collective-permute-done((f32[16,128,128]{2,1,0:T(8,128)}, f32[16,128,128]{2,1,0:T(8,128)S(1)}, u32[]{:S(2)}, u32[]{:S(2)}) %collective-permute-start) | collective-permute-done | bytes 1048608 | tf_op jit(solution)/shard_map/while/body/eval_jaxpr/ppermute | solution.py:14
  186.1 1.4 multiply_add_fusion.2
  187.4 1.9 collective-permute-start
  189.4 20.5 %collective-permute-done = f32[16,128,128]{2,1,0:T(8,128)S(1)} collective-permute-done((f32[16,128,128]{2,1,0:T(8,128)}, f32[16,128,128]{2,1,0:T(8,128)S(1)}, u32[]{:S(2)}, u32[]{:S(2)}) %collective-permute-start) | collective-permute-done | bytes 1048608 | tf_op jit(solution)/shard_map/while/body/eval_jaxpr/ppermute | solution.py:14
  209.8 1.4 multiply_add_fusion.2
  211.2 1.9 collective-permute-start
  213.1 19.5 %collective-permute-done = f32[16,128,128]{2,1,0:T(8,128)S(1)} collective-permute-done((f32[16,128,128]{2,1,0:T(8,128)}, f32[16,128,128]{2,1,0:T(8,128)S(1)}, u32[]{:S(2)}, u32[]{:S(2)}) %collective-permute-start) | collective-permute-done | bytes 1048608 | tf_op jit(solution)/shard_map/while/body/eval_jaxpr/ppermute | solution.py:14
  232.7 1.4 multiply_add_fusion.2
  234.0 1.9 collective-permute-start
  235.9 18.6 %collective-permute-done = f32[16,128,128]{2,1,0:T(8,128)S(1)} collective-permute-done((f32[16,128,128]{2,1,0:T(8,128)}, f32[16,128,128]{2,1,0:T(8,128)S(1)}, u32[]{:S(2)}, u32[]{:S(2)}) %collective-permute-start) | collective-permute-done | bytes 1048608 | tf_op jit(solution)/shard_map/while/body/eval_jaxpr/ppermute | solution.py:14
  255.9 1.9 collective-permute-start
  257.9 18.3 %collective-permute-done = f32[16,128,128]{2,1,0:T(8,128)S(1)} collective-permute-done((f32[16,128,128]{2,1,0:T(8,128)}, f32[16,128,128]{2,1,0:T(8,128)S(1)}, u32[]{:S(2)}, u32[]{:S(2)}) %collective-permute-start) | collective-permute-done | bytes 1048608 | tf_op jit(solution)/shard_map/while/body/eval_jaxpr/ppermute | solution.py:14
  276.2 1.4 multiply_add_fusion.2
  277.6 1.9 collective-permute-start
  279.5 18.3 %collective-permute-done = f32[16,128,128]{2,1,0:T(8,128)S(1)} collective-permute-done((f32[16,128,128]{2,1,0:T(8,128)}, f32[16,128,128]{2,1,0:T(8,128)S(1)}, u32[]{:S(2)}, u32[]{:S(2)}) %collective-permute-start) | collective-permute-done | bytes 1048608 | tf_op jit(solution)/shard_map/while/body/eval_jaxpr/ppermute | solution.py:14
  299.2 1.9 collective-permute-start
  301.1 18.3 %collective-permute-done = f32[16,128,128]{2,1,0:T(8,128)S(1)} collective-permute-done((f32[16,128,128]{2,1,0:T(8,128)}, f32[16,128,128]{2,1,0:T(8,128)S(1)}, u32[]{:S(2)}, u32[]{:S(2)}) %collective-permute-start) | collective-permute-done | bytes 1048608 | tf_op jit(solution)/shard_map/while/body/eval_jaxpr/ppermute | solution.py:14
  319.4 1.4 multiply_add_fusion.2
  320.8 1.9 collective-permute-start
  322.7 18.5 %collective-permute-done = f32[16,128,128]{2,1,0:T(8,128)S(1)} collective-permute-done((f32[16,128,128]{2,1,0:T(8,128)}, f32[16,128,128]{2,1,0:T(8,128)S(1)}, u32[]{:S(2)}, u32[]{:S(2)}) %collective-permute-start) | collective-permute-done | bytes 1048608 | tf_op jit(solution)/shard_map/while/body/eval_jaxpr/ppermute | solution.py:14
  341.2 1.4 multiply_add_fusion.2
  342.6 1.9 collective-permute-start
  344.5 19.5 %collective-permute-done = f32[16,128,128]{2,1,0:T(8,128)S(1)} collective-permute-done((f32[16,128,128]{2,1,0:T(8,128)}, f32[16,128,128]{2,1,0:T(8,128)S(1)}, u32[]{:S(2)}, u32[]{:S(2)}) %collective-permute-start) | collective-permute-done | bytes 1048608 | tf_op jit(solution)/shard_map/while/body/eval_jaxpr/ppermute | solution.py:14
  365.4 1.9 collective-permute-start
  367.3 20.9 %collective-permute-done = f32[16,128,128]{2,1,0:T(8,128)S(1)} collective-permute-done((f32[16,128,128]{2,1,0:T(8,128)}, f32[16,128,128]{2,1,0:T(8,128)S(1)}, u32[]{:S(2)}, u32[]{:S(2)}) %collective-permute-start) | collective-permute-done | bytes 1048608 | tf_op jit(solution)/shard_map/while/body/eval_jaxpr/ppermute | solution.py:14
  388.2 1.4 multiply_add_fusion.2
  389.6 16.2 %while.36 = (s32[]{:T(128)}, f32[16,128,128]{2,1,0:T(8,128)}, bf16[4,16,128,128]{3,2,1,0:T(8,128)(2,1)S(1)}, f32[4,16]{1,0:T(4,128)S(1)}, f32[4,16,128,128]{3,2,1,0:T(8,128)}, /*index=5*/s32[]{:T(128)}) while((s32[]{:T(128)}, f32[16,128,128]{2,1,0:T(8,128)}, bf16[4,16,128,128]{3,2,1,0:T(8,128)(2,1)S(1)}, f32[4,16]{1,0:T(4,128)S(1)}, ...), condition=%wide.region_8.9_spmd, body=%wide.region_7.8_spmd.sunk | while | flops 524290 | bytes 5243153 | solution.py:61
  391.0 2.7 bitcast_add_fusion.4
  395.0 2.7 bitcast_add_fusion.4
  399.1 2.7 bitcast_add_fusion.4
  403.2 2.7 bitcast_add_fusion.4
  408.0 9.4 %fusion.3 = f32[4,256,16,128]{3,1,2,0:T(8,128)S(1)} fusion(f32[4,16,128,256]{2,3,1,0:T(8,128)S(1)} %fusion.27, f32[16]{0:T(128)S(1)} %copy-done.8, f32[4,256,16]{1,2,0:T(8,128)S(1)} %get-tuple-element.155, f32[4,256,256]{2,1,0:T(8,128)S(1)} %fusion.26, f32[16,4,256]{2,0,1:T(8,128)S(1)} %copy_bitcast_fusion, pred[256,256]{1,0:T(8,128)(4,1)S(1)} %iota_compare_fusion, ...), kind=kOutput, calls=%fused_computation.15 | convolution fusion | flops 1105199104 | bytes 22216768 | tf_op jit(solution)/shard_map/hkts,kshp->kthp/dot_general | solution.py:39
  417.4 5.1 %copy.38 = f32[4,256,16,128]{3,2,1,0:T(8,128)S(1)} copy(f32[4,256,16,128]{3,1,2,0:T(8,128)S(1)} %fusion.3) | data formatting | bytes 16777216 | tf_op jit(solution)/shard_map/add | solution.py:69
  422.5 3.2 copy-done.2
  425.7 3.4 multiply_reduce_fusion
  429.1 16.9 %psum.7 = f32[1024]{0:T(1024)S(1)} all-reduce(f32[1024]{0:T(1024)S(1)} %multiply_reduce_fusion), channel_id=1, replica_groups=mesh['seq'=16,'head'=2] {'head'}, use_global_device_ids=true, to_apply=%region_10.11 | all-reduce | flops 1024 | bytes 8192 | tf_op jit(solution)/shard_map/psum | solution.py:72
  446.0 9.6 %multiply_convert_fusion.2 = bf16[1024,2048]{1,0:T(8,128)(2,1)} fusion(f32[2048]{0:T(1024)S(1)} %copy-done.7, f32[1024]{0:T(1024)S(1)} %add_rsqrt_fusion, bf16[1024,2048]{1,0:T(8,128)(2,1)} %param.15, f32[128,8,16,128]{3,2,1,0:T(8,128)} %bitcast.76), kind=kLoop, calls=%fused_computation.22 | loop fusion | flops 18874368 | bytes 16789504 | tf_op jit(solution)/shard_map/convert_element_type | solution.py:73
  (78 shorter events, 14.5 us)
Async XLA Ops:
  0.0 405.8 %copy-start = (bf16[1024,128]{1,0:T(8,128)(2,1)S(1)}, bf16[1024,128]{1,0:T(8,128)(2,1)}, u32[]{:S(2)}) copy-start(bf16[1024,128]{1,0:T(8,128)(2,1)} %param.17) | copy-start | bytes 786436
  0.0 9.5 %copy-start.6 = (bf16[1024,128]{1,0:T(8,128)(2,1)S(1)}, bf16[1024,128]{1,0:T(8,128)(2,1)}, u32[]{:S(2)}) copy-start(bf16[1024,128]{1,0:T(8,128)(2,1)} %param.16) | copy-start | bytes 786436
  7.6 1.9 copy-start.3
  28.2 26.1 %collective-permute-start = (f32[16,128,128]{2,1,0:T(8,128)}, f32[16,128,128]{2,1,0:T(8,128)S(1)}, u32[]{:S(2)}, u32[]{:S(2)}) collective-permute-start(f32[16,128,128]{2,1,0:T(8,128)} %get-tuple-element.268), channel_id=1, source_target_pairs={{0,2},{2,4},{4,6},{6,8},{8,10},{10,12},{12,14},{14,16},{16,18},{18... | collective-permute-start | bytes 3145736 | tf_op jit(solution)/shard_map/while/body/eval_jaxpr/ppermute | solution.py:14
  54.4 1.4 copy-start.1
  55.7 26.1 %collective-permute-start = (f32[16,128,128]{2,1,0:T(8,128)}, f32[16,128,128]{2,1,0:T(8,128)S(1)}, u32[]{:S(2)}, u32[]{:S(2)}) collective-permute-start(f32[16,128,128]{2,1,0:T(8,128)} %get-tuple-element.268), channel_id=1, source_target_pairs={{0,2},{2,4},{4,6},{6,8},{8,10},{10,12},{12,14},{14,16},{16,18},{18... | collective-permute-start | bytes 3145736 | tf_op jit(solution)/shard_map/while/body/eval_jaxpr/ppermute | solution.py:14
  81.8 1.4 copy-start.1
  83.2 26.1 %collective-permute-start = (f32[16,128,128]{2,1,0:T(8,128)}, f32[16,128,128]{2,1,0:T(8,128)S(1)}, u32[]{:S(2)}, u32[]{:S(2)}) collective-permute-start(f32[16,128,128]{2,1,0:T(8,128)} %get-tuple-element.268), channel_id=1, source_target_pairs={{0,2},{2,4},{4,6},{6,8},{8,10},{10,12},{12,14},{14,16},{16,18},{18... | collective-permute-start | bytes 3145736 | tf_op jit(solution)/shard_map/while/body/eval_jaxpr/ppermute | solution.py:14
  109.3 1.4 copy-start.1
  110.6 25.1 %collective-permute-start = (f32[16,128,128]{2,1,0:T(8,128)}, f32[16,128,128]{2,1,0:T(8,128)S(1)}, u32[]{:S(2)}, u32[]{:S(2)}) collective-permute-start(f32[16,128,128]{2,1,0:T(8,128)} %get-tuple-element.268), channel_id=1, source_target_pairs={{0,2},{2,4},{4,6},{6,8},{8,10},{10,12},{12,14},{14,16},{16,18},{18... | collective-permute-start | bytes 3145736 | tf_op jit(solution)/shard_map/while/body/eval_jaxpr/ppermute | solution.py:14
  135.8 1.4 copy-start.1
  137.2 24.2 %collective-permute-start = (f32[16,128,128]{2,1,0:T(8,128)}, f32[16,128,128]{2,1,0:T(8,128)S(1)}, u32[]{:S(2)}, u32[]{:S(2)}) collective-permute-start(f32[16,128,128]{2,1,0:T(8,128)} %get-tuple-element.268), channel_id=1, source_target_pairs={{0,2},{2,4},{4,6},{6,8},{8,10},{10,12},{12,14},{14,16},{16,18},{18... | collective-permute-start | bytes 3145736 | tf_op jit(solution)/shard_map/while/body/eval_jaxpr/ppermute | solution.py:14
  161.4 1.4 copy-start.1
  162.8 23.3 %collective-permute-start = (f32[16,128,128]{2,1,0:T(8,128)}, f32[16,128,128]{2,1,0:T(8,128)S(1)}, u32[]{:S(2)}, u32[]{:S(2)}) collective-permute-start(f32[16,128,128]{2,1,0:T(8,128)} %get-tuple-element.268), channel_id=1, source_target_pairs={{0,2},{2,4},{4,6},{6,8},{8,10},{10,12},{12,14},{14,16},{16,18},{18... | collective-permute-start | bytes 3145736 | tf_op jit(solution)/shard_map/while/body/eval_jaxpr/ppermute | solution.py:14
  186.1 1.4 copy-start.1
  187.4 22.4 %collective-permute-start = (f32[16,128,128]{2,1,0:T(8,128)}, f32[16,128,128]{2,1,0:T(8,128)S(1)}, u32[]{:S(2)}, u32[]{:S(2)}) collective-permute-start(f32[16,128,128]{2,1,0:T(8,128)} %get-tuple-element.268), channel_id=1, source_target_pairs={{0,2},{2,4},{4,6},{6,8},{8,10},{10,12},{12,14},{14,16},{16,18},{18... | collective-permute-start | bytes 3145736 | tf_op jit(solution)/shard_map/while/body/eval_jaxpr/ppermute | solution.py:14
  209.8 1.4 copy-start.1
  211.2 21.5 %collective-permute-start = (f32[16,128,128]{2,1,0:T(8,128)}, f32[16,128,128]{2,1,0:T(8,128)S(1)}, u32[]{:S(2)}, u32[]{:S(2)}) collective-permute-start(f32[16,128,128]{2,1,0:T(8,128)} %get-tuple-element.268), channel_id=1, source_target_pairs={{0,2},{2,4},{4,6},{6,8},{8,10},{10,12},{12,14},{14,16},{16,18},{18... | collective-permute-start | bytes 3145736 | tf_op jit(solution)/shard_map/while/body/eval_jaxpr/ppermute | solution.py:14
  232.7 1.4 copy-start.1
  234.0 20.5 %collective-permute-start = (f32[16,128,128]{2,1,0:T(8,128)}, f32[16,128,128]{2,1,0:T(8,128)S(1)}, u32[]{:S(2)}, u32[]{:S(2)}) collective-permute-start(f32[16,128,128]{2,1,0:T(8,128)} %get-tuple-element.268), channel_id=1, source_target_pairs={{0,2},{2,4},{4,6},{6,8},{8,10},{10,12},{12,14},{14,16},{16,18},{18... | collective-permute-start | bytes 3145736 | tf_op jit(solution)/shard_map/while/body/eval_jaxpr/ppermute | solution.py:14
  254.6 1.4 copy-start.1
  255.9 20.2 %collective-permute-start = (f32[16,128,128]{2,1,0:T(8,128)}, f32[16,128,128]{2,1,0:T(8,128)S(1)}, u32[]{:S(2)}, u32[]{:S(2)}) collective-permute-start(f32[16,128,128]{2,1,0:T(8,128)} %get-tuple-element.268), channel_id=1, source_target_pairs={{0,2},{2,4},{4,6},{6,8},{8,10},{10,12},{12,14},{14,16},{16,18},{18... | collective-permute-start | bytes 3145736 | tf_op jit(solution)/shard_map/while/body/eval_jaxpr/ppermute | solution.py:14
  276.2 1.4 copy-start.1
  277.6 20.2 %collective-permute-start = (f32[16,128,128]{2,1,0:T(8,128)}, f32[16,128,128]{2,1,0:T(8,128)S(1)}, u32[]{:S(2)}, u32[]{:S(2)}) collective-permute-start(f32[16,128,128]{2,1,0:T(8,128)} %get-tuple-element.268), channel_id=1, source_target_pairs={{0,2},{2,4},{4,6},{6,8},{8,10},{10,12},{12,14},{14,16},{16,18},{18... | collective-permute-start | bytes 3145736 | tf_op jit(solution)/shard_map/while/body/eval_jaxpr/ppermute | solution.py:14
  297.8 1.4 copy-start.1
  299.2 20.2 %collective-permute-start = (f32[16,128,128]{2,1,0:T(8,128)}, f32[16,128,128]{2,1,0:T(8,128)S(1)}, u32[]{:S(2)}, u32[]{:S(2)}) collective-permute-start(f32[16,128,128]{2,1,0:T(8,128)} %get-tuple-element.268), channel_id=1, source_target_pairs={{0,2},{2,4},{4,6},{6,8},{8,10},{10,12},{12,14},{14,16},{16,18},{18... | collective-permute-start | bytes 3145736 | tf_op jit(solution)/shard_map/while/body/eval_jaxpr/ppermute | solution.py:14
  319.4 1.4 copy-start.1
  320.8 20.4 %collective-permute-start = (f32[16,128,128]{2,1,0:T(8,128)}, f32[16,128,128]{2,1,0:T(8,128)S(1)}, u32[]{:S(2)}, u32[]{:S(2)}) collective-permute-start(f32[16,128,128]{2,1,0:T(8,128)} %get-tuple-element.268), channel_id=1, source_target_pairs={{0,2},{2,4},{4,6},{6,8},{8,10},{10,12},{12,14},{14,16},{16,18},{18... | collective-permute-start | bytes 3145736 | tf_op jit(solution)/shard_map/while/body/eval_jaxpr/ppermute | solution.py:14
  341.2 1.4 copy-start.1
  342.6 21.5 %collective-permute-start = (f32[16,128,128]{2,1,0:T(8,128)}, f32[16,128,128]{2,1,0:T(8,128)S(1)}, u32[]{:S(2)}, u32[]{:S(2)}) collective-permute-start(f32[16,128,128]{2,1,0:T(8,128)} %get-tuple-element.268), channel_id=1, source_target_pairs={{0,2},{2,4},{4,6},{6,8},{8,10},{10,12},{12,14},{14,16},{16,18},{18... | collective-permute-start | bytes 3145736 | tf_op jit(solution)/shard_map/while/body/eval_jaxpr/ppermute | solution.py:14
  364.0 1.4 copy-start.1
  365.4 22.8 %collective-permute-start = (f32[16,128,128]{2,1,0:T(8,128)}, f32[16,128,128]{2,1,0:T(8,128)S(1)}, u32[]{:S(2)}, u32[]{:S(2)}) collective-permute-start(f32[16,128,128]{2,1,0:T(8,128)} %get-tuple-element.268), channel_id=1, source_target_pairs={{0,2},{2,4},{4,6},{6,8},{8,10},{10,12},{12,14},{14,16},{16,18},{18... | collective-permute-start | bytes 3145736 | tf_op jit(solution)/shard_map/while/body/eval_jaxpr/ppermute | solution.py:14
  388.2 1.4 copy-start.1
  405.8 2.2 copy-start.4
  405.8 2.2 copy-start.8
  417.4 8.3 %copy-start.5 = (bf16[1024,2048]{1,0:T(8,128)(2,1)S(1)}, bf16[1024,2048]{1,0:T(8,128)(2,1)}, u32[]{:S(2)}) copy-start(bf16[1024,2048]{1,0:T(8,128)(2,1)} %param.15) | copy-start | bytes 12582916
  422.5 3.2 copy-start.2
  422.5 23.5 %copy-start.7 = (f32[2048]{0:T(1024)S(1)}, f32[2048]{0:T(1024)}, u32[]{:S(2)}) copy-start(f32[2048]{0:T(1024)} %param.21) | copy-start | bytes 24580
where the time goes:
time: 460 us; the launch traced here: 456 us
  waiting for transfers between devices  305 us (66%)
  other arithmetic  53.7 us (12%)
  starting transfers between devices  35.6 us (8%)
  local copies, waits for them, and re-layouts  26.6 us (6%)
  matrix products  17.4 us (4%)
  blocking collectives  16.9 us (4%)
    ppermute x15, waiting for transfers between devices, passed_along(): return lax.ppermute(block, axis, route)  305 us
    ppermute x15, starting transfers between devices, passed_along(): return lax.ppermute(block, axis, route)  35.6 us
    add x15, other arithmetic, relay_turn(): return (received, device_decay[:, None, None] * received + summary)  20.6 us
    psum x1, blocking collectives, local(): lax.psum(jnp.sum(gated_out * gated_out, axis=1), 'head')  16.9 us
    add x8, other arithmetic, advance(): return (decay_part[:, None, None] * running + state_part, running)  16.4 us
    unnamed x19, local copies, waits for them, and re-layouts  15.8 us
    convert_element_type x1, other arithmetic, local(): (gated_out * lax.rsqrt(row_power[:, None] + 1e-05) * norm_gain[None, :])....  9.62 us
    dot_general x1, matrix products, local(): jnp.einsum('hkts,kshp->kthp', mixing, x_blocks, preferred_element_type=jn...  9.36 us
  transfers between devices with their start and end apart: 15, of which 15 were waited for; matrix products, arithmetic and copies ran while one was open for 0% of the time, Pallas kernels for 0%

commit v1 on v0

v1 whole, which is shorter than its diff:
```python
import functools

import jax
import jax.numpy as jnp
from jax import lax
from jax.experimental import pallas as pl
from jax.experimental.pallas import tpu as pltpu
from jax.sharding import PartitionSpec as P

HEAD_DIM = 128
GROUP = 256
TEAM = 4
CHUNKS = 4
F32 = jnp.float32
MESH = pl.DeviceIdType.MESH


def dot(a, b, dims=((1,), (0,)), **kw):
    return lax.dot_general(a, b, (dims, ((), ())), preferred_element_type=F32, **kw)


def spread_lanes(columns, heads):
    rows = columns.shape[0]
    return jnp.concatenate(
        [jnp.broadcast_to(columns[:, h : h + 1], (rows, HEAD_DIM)) for h in range(heads)], axis=1
    )


def kernel(
    sections, groups, x_ref, g_ref, b_ref, c_ref, codes_ref, rate_ref, skip_ref, gain_ref, out_ref,
    cumc, cumr, ends, decay, total_decay, states, scores, y, sums, got, prefix, turns, enter_z,
    next_z, send_e, incoming, power, power_in, send1, recv1, send2, recv2, send3, recv3, send4, recv4,
):
    rows, width = x_ref.shape
    heads = codes_ref.shape[0]
    blocks = rows // GROUP
    part = heads // TEAM
    lanes = part * HEAD_DIM
    state = b_ref.shape[1]
    teams = sections // TEAM
    seq = lax.axis_index("seq")
    core = lax.axis_index("head")
    z, q = seq // TEAM, seq % TEAM
    mates = [z * TEAM + (q + i) % TEAM for i in range(1, TEAM)]
    step = state // CHUNKS

    barrier = pltpu.get_barrier_semaphore()
    for mate in mates:
        pl.semaphore_signal(barrier, inc=1, device_id={"seq": mate}, device_id_type=MESH)
    for i in range(1, groups):
        other = (core + i) % groups
        pl.semaphore_signal(barrier, inc=1, device_id={"head": other}, device_id_type=MESH)

    @pl.when(z > 0)
    def _():
        pl.semaphore_signal(barrier, inc=1, device_id={"seq": seq - TEAM}, device_id_type=MESH)

    @pl.when(z < teams - 1)
    def _():
        pl.semaphore_signal(barrier, inc=1, device_id={"seq": seq + TEAM}, device_id_type=MESH)

    def lane_slice(p):
        return pl.ds(pl.multiple_of(p * lanes, lanes), lanes)

    def row_slice(k):
        return pl.ds(pl.multiple_of(k * GROUP, GROUP), GROUP)

    t_at = lax.broadcasted_iota(jnp.int32, (GROUP, GROUP), 0)
    s_at = lax.broadcasted_iota(jnp.int32, (GROUP, GROUP), 1)
    upto = jnp.where(t_at <= s_at, 1.0, 0.0).astype(F32)
    for k in range(blocks):
        logs = -(codes_ref[:, k * GROUP : (k + 1) * GROUP].astype(F32) * rate_ref[...])
        logs = logs / (8.0 * rows * sections)
        cum = dot(logs, upto, precision=lax.Precision.HIGHEST)
        cum_t = cum.T
        for p in range(TEAM):
            cumc[k, p] = cum_t[:, p * part : (p + 1) * part]
            cumr[k, p, :part] = cum[p * part : (p + 1) * part]
        last = jnp.broadcast_to(cum[:, GROUP - 1 : GROUP], (heads, HEAD_DIM))
        for h in range(heads):
            ends[k, :, h * HEAD_DIM : (h + 1) * HEAD_DIM] = last[h : h + 1]
    decay[...] = jnp.exp(ends[...])
    total_decay[...] = jnp.exp(jnp.sum(ends[...], axis=0))

    def summarize(p, carry):
        at = lane_slice(p)
        run = jnp.zeros((state, lanes), F32)
        for k in range(blocks):
            col = cumc[k, p]
            tail = spread_lanes(jnp.exp(col[GROUP - 1 : GROUP] - col), part)
            own = slice(k * GROUP, (k + 1) * GROUP)
            weighted = (tail * x_ref[own, at].astype(F32)).astype(jnp.bfloat16)
            block_state = dot(b_ref[own, :], weighted, ((0,), (0,)))
            states[k, p] = block_state
            run = decay[k, :, at] * run + block_state
        sums[p, :state] = run
        sums[p, state:] = jnp.broadcast_to(total_decay[:, at], (8, lanes))
        return carry

    def to_owner(i):
        mate = (q + i) % TEAM
        return pltpu.make_async_remote_copy(
            src_ref=sums.at[mate], dst_ref=got.at[q], send_sem=send1.at[i - 1],
            recv_sem=recv1.at[i - 1], device_id={"seq": z * TEAM + mate}, device_id_type=MESH,
        )

    def first(i, carry):
        summarize((q + i) % TEAM, 0)

        @pl.when(i == 1)
        def _():
            behind = (z + teams - 1) // teams
            ahead = (2 * teams - 2 - z) // teams
            pl.semaphore_wait(barrier, TEAM - 1 + groups - 1 + behind + ahead)

        to_owner(i).start()
        return carry

    lax.fori_loop(1, TEAM, first, 0)
    summarize(q, 0)
    got[q] = sums[q]

    def score(k, carry):
        at = row_slice(k)
        full = dot(c_ref[at, :], b_ref[at, :], ((1,), (1,)))
        scores[k] = jnp.where(t_at >= s_at, full, 0.0)
        return carry

    lax.fori_loop(0, blocks, score, 0)
    half = GROUP // 2

    def inner(u, carry):
        k, p = u // TEAM, u % TEAM
        start = pl.multiple_of(k * GROUP, GROUP)
        for h in range(part):
            at = pl.ds(pl.multiple_of(p * lanes + h * HEAD_DIM, HEAD_DIM), HEAD_DIM)
            xs = x_ref[pl.ds(start, GROUP), at]
            skip = skip_ref[:, at]
            for r, cols in ((0, half), (half, GROUP)):
                spread = cumc[k, p, r : r + half, h : h + 1] - cumr[k, p, h : h + 1, :cols]
                mixing = jnp.exp(jnp.minimum(spread, 0.0)) * scores[k, r : r + half, :cols]
                got_out = dot(mixing.astype(jnp.bfloat16), xs[:cols])
                y[pl.ds(start + r, half), at] = got_out + skip * xs[r : r + half].astype(F32)
        return carry

    units = blocks * TEAM
    before = jnp.minimum(6 + 3 * z, units)
    lax.fori_loop(0, before, inner, 0)

    for i in range(1, TEAM):
        to_owner(i).wait()
    run = jnp.zeros((state, lanes), F32)
    through = jnp.ones((1, lanes), F32)
    for j in range(TEAM):
        prefix[j] = run
        turns[j] = jnp.broadcast_to(through, (8, lanes))
        run = got[j, state : state + 1] * run + got[j, :state]
        through = through * got[j, state : state + 1]
    prefix[TEAM] = run
    turns[TEAM] = jnp.broadcast_to(through, (8, lanes))

    @pl.when(z == 0)
    def _():
        enter_z[...] = jnp.zeros_like(enter_z)

    def along(c):
        at = pl.ds(pl.multiple_of(c * step, step), step)
        return pltpu.make_async_remote_copy(
            src_ref=next_z.at[at], dst_ref=enter_z.at[at], send_sem=send2.at[c],
            recv_sem=recv2.at[c], device_id={"seq": seq + TEAM}, device_id_type=MESH,
        )

    def to_mate(c, i):
        at = pl.ds(pl.multiple_of(c * step, step), step)
        mate = (q + i) % TEAM
        return pltpu.make_async_remote_copy(
            src_ref=send_e.at[mate, at], dst_ref=incoming.at[q, at], send_sem=send3.at[c, i - 1],
            recv_sem=recv3.at[c, i - 1], device_id={"seq": z * TEAM + mate}, device_id_type=MESH,
        )

    def hand_on(c, carry):
        at = pl.ds(pl.multiple_of(c * step, step), step)

        @pl.when(z > 0)
        def _():
            along(c).wait_recv()

        arrived = enter_z[at, :]

        @pl.when(z < teams - 1)
        def _():
            next_z[at, :] = turns[TEAM, :1] * arrived + prefix[TEAM, at, :]
            along(c).start()

        for j in range(TEAM):
            send_e[j, at, :] = turns[j, :1] * arrived + prefix[j, at, :]
        for i in range(1, TEAM):
            to_mate(c, i).start()
        return carry

    lax.fori_loop(0, CHUNKS, hand_on, 0)
    incoming[q] = send_e[q]
    lax.fori_loop(before, units, inner, 0)
    power[...] = jnp.zeros_like(power)

    def finish(p):
        at = lane_slice(p)

        def block(k, run):
            own = row_slice(k)
            read = dot(c_ref[own, :], run.astype(jnp.bfloat16))
            value = y[own, at] + spread_lanes(jnp.exp(cumc[k, p]), part) * read
            gate = g_ref[own, at].astype(F32)
            value = value * (gate / (1.0 + jnp.exp(-gate)))
            y[own, at] = value
            square = value * value
            folded = square[:, :HEAD_DIM]
            for h in range(1, part):
                folded = folded + square[:, h * HEAD_DIM : (h + 1) * HEAD_DIM]
            power[own, :] += folded
            return decay[k, :, at] * run + states[k, p]

        lax.fori_loop(0, blocks, block, incoming[p])

    finish(q)

    def rest(i, carry):
        for c in range(CHUNKS):
            to_mate(c, i).wait_recv()
        finish((q + TEAM - i) % TEAM)
        return carry

    lax.fori_loop(1, TEAM, rest, 0)

    def swap(i):
        return pltpu.make_async_remote_copy(
            src_ref=power, dst_ref=power_in.at[i - 1], send_sem=send4.at[i - 1],
            recv_sem=recv4.at[i - 1], device_id={"head": (core + i) % groups}, device_id_type=MESH,
        )

    for i in range(1, groups):
        swap(i).start()
    for c in range(CHUNKS):
        for i in range(1, TEAM):
            to_mate(c, i).wait_send()

    @pl.when(z < teams - 1)
    def _():
        for c in range(CHUNKS):
            along(c).wait_send()

    for i in range(1, groups):
        swap(i).wait()

    def norm(k, carry):
        own = row_slice(k)
        total = power[own, :]
        for i in range(groups - 1):
            total = total + power_in[i, own, :]
        mean = jnp.sum(total, axis=1, keepdims=True) / (groups * width)
        scale = lax.rsqrt(mean + 1e-05)
        for p in range(TEAM):
            at = slice(p * lanes, (p + 1) * lanes)
            out_ref[own, at] = (y[own, at] * scale * gain_ref[:, at]).astype(jnp.bfloat16)
        return carry

    lax.fori_loop(0, blocks, norm, 0)


def local(
    sections, groups, ssm_input, gate_input, write_proj, read_proj, decay_codes, decay_rate, skip_gain, norm_gain
):
    rows, width = ssm_input.shape
    heads = decay_rate.shape[0]
    state = write_proj.shape[1]
    blocks = rows // GROUP
    part = heads // TEAM
    lanes = part * HEAD_DIM
    in_vmem = pl.BlockSpec(memory_space=pltpu.VMEM)
    dma = pltpu.SemaphoreType.DMA
    return pl.pallas_call(
        functools.partial(kernel, sections, groups),
        out_shape=jax.ShapeDtypeStruct((rows, width), jnp.bfloat16),
        in_specs=[in_vmem] * 8,
        out_specs=in_vmem,
        scratch_shapes=[
            pltpu.VMEM((blocks, TEAM, GROUP, part), F32),
            pltpu.VMEM((blocks, TEAM, 8, GROUP), F32),
            pltpu.VMEM((blocks, 1, width), F32),
            pltpu.VMEM((blocks, 1, width), F32),
            pltpu.VMEM((1, width), F32),
            pltpu.VMEM((blocks, TEAM, state, lanes), F32),
            pltpu.VMEM((blocks, GROUP, GROUP), F32),
            pltpu.VMEM((rows, width), F32),
            pltpu.VMEM((TEAM, state + 8, lanes), F32),
            pltpu.VMEM((TEAM, state + 8, lanes), F32),
            pltpu.VMEM((TEAM + 1, state, lanes), F32),
            pltpu.VMEM((TEAM + 1, 8, lanes), F32),
            pltpu.VMEM((state, lanes), F32),
            pltpu.VMEM((state, lanes), F32),
            pltpu.VMEM((TEAM, state, lanes), F32),
            pltpu.VMEM((TEAM, state, lanes), F32),
            pltpu.VMEM((rows, HEAD_DIM), F32),
            pltpu.VMEM((groups - 1, rows, HEAD_DIM), F32),
            dma((TEAM - 1,)),
            dma((TEAM - 1,)),
            dma((CHUNKS,)),
            dma((CHUNKS,)),
            dma((CHUNKS, TEAM - 1)),
            dma((CHUNKS, TEAM - 1)),
            dma((groups - 1,)),
            dma((groups - 1,)),
        ],
        compiler_params=pltpu.CompilerParams(
            collective_id=0, has_side_effects=True, vmem_limit_bytes=56 * 1024 * 1024
        ),
    )(
        ssm_input, gate_input, write_proj, read_proj, decay_codes, decay_rate[:, None],
        jnp.repeat(skip_gain, HEAD_DIM)[None, :], norm_gain[None, :],
    )


def solution(mesh):
    placed = (
        P("seq", "head"),
        P("seq", "head"),
        P("seq", None),
        P("seq", None),
        P("head", "seq"),
        P("head"),
        P("head"),
        P("head"),
    )
    return jax.shard_map(
        functools.partial(local, mesh.shape["seq"], mesh.shape["head"]),
        mesh=mesh, in_specs=placed, out_specs=P("seq", "head"), check_vma=False,
    )
```

time: 460 us -> 56.9 us (0.12)
  waiting for transfers between devices: 305 us -> 0 us
  other arithmetic: 53.7 us -> 0 us
  Pallas kernels: 0 us -> 49.3 us
  starting transfers between devices: 35.6 us -> 0 us
  local copies, waits for them, and re-layouts: 26.6 us -> 7.44 us
  matrix products: 17.4 us -> 0 us
  blocking collectives: 16.9 us -> 0 us
    ppermute x15 -> x0, waiting for transfers between devices: 305 us -> none  [passed_along(): return lax.ppermute(block, axis, route)]
    pallas_call x0 -> x1, Pallas kernels: none -> 49.3 us  [local(): pl.pallas_call(functools.partial(kernel, sections, groups), out_shape=jax...]
    add x23 -> x0, other arithmetic: 37 us -> none  [the longest x15 20.6 us: relay_turn(): return (received, device_decay[:, None, None] * received + summary)]
    ppermute x15 -> x0, starting transfers between devices: 35.6 us -> none  [passed_along(): return lax.ppermute(block, axis, route)]
    dot_general x4 -> x0, matrix products: 17.4 us -> none  [the longest x1 9.36 us: local(): jnp.einsum('hkts,kshp->kthp', mixing, x_blocks, preferred_element_type=jn...]
    psum x1 -> x0, blocking collectives: 16.9 us -> none  [local(): lax.psum(jnp.sum(gated_out * gated_out, axis=1), 'head')]
    unnamed x19 -> x1, local copies, waits for them, and re-layouts: 15.8 us -> 4.79 us
    convert_element_type x1 -> x0, other arithmetic: 9.62 us -> none  [local(): (gated_out * lax.rsqrt(row_power[:, None] + 1e-05) * norm_gain[None, :])....]
  transfers between devices with their start and end apart: 15 -> 0, of which waited for: 15 -> 0; matrix products, arithmetic and copies ran while one was open for 0% -> 0% of each run, Pallas kernels for 0% -> 0%
where the time goes in v1:
time: 56.9 us; the launch traced here: 56.8 us
  Pallas kernels  49.3 us (87%)
  local copies, waits for them, and re-layouts  7.44 us (13%)
    pallas_call x1, Pallas kernels, local(): pl.pallas_call(functools.partial(kernel, sections, groups), out_shape=jax...  49.3 us
    unnamed x1, local copies, waits for them, and re-layouts  4.79 us
    broadcast_in_dim x1, local copies, waits for them, and re-layouts, local(): decay_rate[:, None]  1.33 us
    broadcast_in_dim x1, local copies, waits for them, and re-layouts, local(): jnp.repeat(skip_gain, HEAD_DIM)[None, :]  1.32 us

profile of v1, /device:TPU:27, one launch (start us, length us, event | category | flops | bytes accessed | tf_op | source)
XLA Modules:
  0.0 56.8 jit_solution(18310566030501826134)
XLA Ops:
  0.0 1.3 %copy.9.rate_ref = f32[16,1]{1,0:T(8,128)} copy(f32[16,1]{0,1:T(1,128)} %bitcast.5) | data formatting | bytes 128 | tf_op jit(solution)/shard_map/broadcast_in_dim | solution.py:318
  1.3 1.3 %broadcast_in_dim.10 = f32[16,128]{1,0:T(8,128)} broadcast(f32[16]{0:T(128)} %param.14), dimensions={0} | broadcast | bytes 8256 | tf_op jit(solution)/shard_map/broadcast_in_dim | solution.py:319
  2.6 49.3 %shard_map.82 = bf16[1024,2048]{1,0:T(8,128)(2,1)} custom-call(bf16[1024,2048]{1,0:T(8,128)(2,1)} %x_ref.1, bf16[1024,2048]{1,0:T(8,128)(2,1)} %g_ref.1, bf16[1024,128]{1,0:T(8,128)(2,1)} %b_ref.1, bf16[1024,128]{1,0:T(8,128)(2,1)} %c_ref.1, s32[16,1024]{1,0:T(8,128)} %codes_ref.1, f32[16,1]{1,0:T(8,128)} %copy.9.rate_ref, f32[1,2048]{1,0:T(1,128)} %bitcast.3, ...), custom_call_target="tpu_custom_call" | custom-call | tf_op jit(solution)/shard_map/pallas_call | solution.py:281
  52.0 4.8 %copy.11 = bf16[1024,2048]{1,0:T(8,128)(2,1)} copy(bf16[1024,2048]{1,0:T(8,128)(2,1)} %shard_map.82) | data formatting | bytes 8388608

commit v2 on v1

--- a/solution.py
+++ b/solution.py
@@ -27,11 +27,12 @@
 
 
 def kernel(
-    sections, groups, x_ref, g_ref, b_ref, c_ref, codes_ref, rate_ref, skip_ref, gain_ref, out_ref,
-    cumc, cumr, ends, decay, total_decay, states, scores, y, sums, got, prefix, turns, enter_z,
+    sections, groups, x_hbm, g_hbm, b_ref, c_ref, codes_ref, rate_ref, skip_ref, out_hbm, scale_ref,
+    x_ref, g_ref, gated, carry_gain, skip_row,    cumc, cumr, ends, decay, total_decay, states, scores, y, sums, got, prefix, turns, enter_z,
     next_z, send_e, incoming, power, power_in, send1, recv1, send2, recv2, send3, recv3, send4, recv4,
+    load_x, load_g, store,
 ):
-    rows, width = x_ref.shape
+    rows, width = x_hbm.shape
     heads = codes_ref.shape[0]
     blocks = rows // GROUP
     part = heads // TEAM
@@ -44,6 +45,25 @@
     mates = [z * TEAM + (q + i) % TEAM for i in range(1, TEAM)]
     step = state // CHUNKS
 
+    def lane_slice(p):
+        return pl.ds(pl.multiple_of(p * lanes, lanes), lanes)
+
+    def row_slice(k):
+        return pl.ds(pl.multiple_of(k * GROUP, GROUP), GROUP)
+
+    def fetch_x(i):
+        at = lane_slice((q + i) % TEAM)
+        return pltpu.make_async_copy(x_hbm.at[:, at], x_ref.at[:, at], load_x.at[i % TEAM])
+
+    def put(p):
+        at = lane_slice(p)
+        return pltpu.make_async_copy(gated.at[:, at], out_hbm.at[:, at], store.at[p])
+
+    fetch_g = pltpu.make_async_copy(g_hbm, g_ref, load_g)
+    for i in range(1, TEAM + 1):
+        fetch_x(i).start()
+    fetch_g.start()
+
     barrier = pltpu.get_barrier_semaphore()
     for mate in mates:
         pl.semaphore_signal(barrier, inc=1, device_id={"seq": mate}, device_id_type=MESH)
@@ -59,17 +79,15 @@
     def _():
         pl.semaphore_signal(barrier, inc=1, device_id={"seq": seq + TEAM}, device_id_type=MESH)
 
-    def lane_slice(p):
-        return pl.ds(pl.multiple_of(p * lanes, lanes), lanes)
-
-    def row_slice(k):
-        return pl.ds(pl.multiple_of(k * GROUP, GROUP), GROUP)
-
     t_at = lax.broadcasted_iota(jnp.int32, (GROUP, GROUP), 0)
     s_at = lax.broadcasted_iota(jnp.int32, (GROUP, GROUP), 1)
     upto = jnp.where(t_at <= s_at, 1.0, 0.0).astype(F32)
+    own_row = lax.broadcasted_iota(jnp.int32, (heads, heads), 0)
+    own_col = lax.broadcasted_iota(jnp.int32, (heads, heads), 1)
+    rate = jnp.sum(jnp.where(own_row == own_col, rate_ref[...], 0.0), axis=1, keepdims=True)
+    skip_row[...] = spread_lanes(skip_ref[...], heads)
     for k in range(blocks):
-        logs = -(codes_ref[:, k * GROUP : (k + 1) * GROUP].astype(F32) * rate_ref[...])
+        logs = -(codes_ref[:, k * GROUP : (k + 1) * GROUP].astype(F32) * rate)
         logs = logs / (8.0 * rows * sections)
         cum = dot(logs, upto, precision=lax.Precision.HIGHEST)
         cum_t = cum.T
@@ -105,6 +123,7 @@
         )
 
     def first(i, carry):
+        fetch_x(i).wait()
         summarize((q + i) % TEAM, 0)
 
         @pl.when(i == 1)
@@ -117,6 +136,7 @@
         return carry
 
     lax.fori_loop(1, TEAM, first, 0)
+    fetch_x(TEAM).wait()
     summarize(q, 0)
     got[q] = sums[q]
 
@@ -128,19 +148,25 @@
 
     lax.fori_loop(0, blocks, score, 0)
     half = GROUP // 2
+    fetch_g.wait()
 
     def inner(u, carry):
         k, p = u // TEAM, u % TEAM
         start = pl.multiple_of(k * GROUP, GROUP)
+        reach = jnp.exp(cumc[k, p])
         for h in range(part):
             at = pl.ds(pl.multiple_of(p * lanes + h * HEAD_DIM, HEAD_DIM), HEAD_DIM)
             xs = x_ref[pl.ds(start, GROUP), at]
-            skip = skip_ref[:, at]
+            skip = skip_row[:, at]
             for r, cols in ((0, half), (half, GROUP)):
                 spread = cumc[k, p, r : r + half, h : h + 1] - cumr[k, p, h : h + 1, :cols]
                 mixing = jnp.exp(jnp.minimum(spread, 0.0)) * scores[k, r : r + half, :cols]
                 got_out = dot(mixing.astype(jnp.bfloat16), xs[:cols])
-                y[pl.ds(start + r, half), at] = got_out + skip * xs[r : r + half].astype(F32)
+                here = pl.ds(pl.multiple_of(start + r, half), half)
+                gate = g_ref[here, at].astype(F32)
+                gate = gate * (0.5 * jnp.tanh(0.5 * gate) + 0.5)
+                y[here, at] = (got_out + skip * xs[r : r + half].astype(F32)) * gate
+                carry_gain[here, at] = reach[r : r + half, h : h + 1] * gate
         return carry
 
     units = blocks * TEAM
@@ -209,10 +235,8 @@
         def block(k, run):
             own = row_slice(k)
             read = dot(c_ref[own, :], run.astype(jnp.bfloat16))
-            value = y[own, at] + spread_lanes(jnp.exp(cumc[k, p]), part) * read
-            gate = g_ref[own, at].astype(F32)
-            value = value * (gate / (1.0 + jnp.exp(-gate)))
-            y[own, at] = value
+            value = y[own, at] + carry_gain[own, at] * read
+            gated[own, at] = value.astype(jnp.bfloat16)
             square = value * value
             folded = square[:, :HEAD_DIM]
             for h in range(1, part):
@@ -221,6 +245,7 @@
             return decay[k, :, at] * run + states[k, p]
 
         lax.fori_loop(0, blocks, block, incoming[p])
+        put(p).start()
 
     finish(q)
 
@@ -258,13 +283,20 @@
         for i in range(groups - 1):
             total = total + power_in[i, own, :]
         mean = jnp.sum(total, axis=1, keepdims=True) / (groups * width)
-        scale = lax.rsqrt(mean + 1e-05)
-        for p in range(TEAM):
-            at = slice(p * lanes, (p + 1) * lanes)
-            out_ref[own, at] = (y[own, at] * scale * gain_ref[:, at]).astype(jnp.bfloat16)
+        scale_ref[own, :] = jnp.broadcast_to(lax.rsqrt(mean + 1e-05), (GROUP, HEAD_DIM))
         return carry
 
     lax.fori_loop(0, blocks, norm, 0)
+    for p in range(TEAM):
+        put(p).wait()
+
+
+def apply_norm(gated_ref, scale_ref, gain_ref, out_ref):
+    scale = scale_ref[...]
+    for at in range(0, gated_ref.shape[1], HEAD_DIM):
+        own = slice(at, at + HEAD_DIM)
+        value = gated_ref[:, own].astype(F32) * scale * gain_ref[:, own]
+        out_ref[:, own] = value.astype(jnp.bfloat16)
 
 
 def local(
@@ -278,12 +310,21 @@
     lanes = part * HEAD_DIM
     in_vmem = pl.BlockSpec(memory_space=pltpu.VMEM)
     dma = pltpu.SemaphoreType.DMA
-    return pl.pallas_call(
+    in_place = pl.BlockSpec(memory_space=pl.ANY)
+    gated, scale = pl.pallas_call(
         functools.partial(kernel, sections, groups),
-        out_shape=jax.ShapeDtypeStruct((rows, width), jnp.bfloat16),
-        in_specs=[in_vmem] * 8,
-        out_specs=in_vmem,
+        out_shape=(
+            jax.ShapeDtypeStruct((rows, width), jnp.bfloat16),
+            jax.ShapeDtypeStruct((rows, HEAD_DIM), F32),
+        ),
+        in_specs=[in_place] * 2 + [in_vmem] * 5,
+        out_specs=(in_place, in_vmem),
         scratch_shapes=[
+            pltpu.VMEM((rows, width), jnp.bfloat16),
+            pltpu.VMEM((rows, width), jnp.bfloat16),
+            pltpu.VMEM((rows, width), jnp.bfloat16),
+            pltpu.VMEM((rows, width), F32),
+            pltpu.VMEM((1, width), F32),
             pltpu.VMEM((blocks, TEAM, GROUP, part), F32),
             pltpu.VMEM((blocks, TEAM, 8, GROUP), F32),
             pltpu.VMEM((blocks, 1, width), F32),
@@ -310,14 +351,30 @@
             dma((CHUNKS, TEAM - 1)),
             dma((groups - 1,)),
             dma((groups - 1,)),
+            dma((TEAM,)),
+            dma,
+            dma((TEAM,)),
         ],
         compiler_params=pltpu.CompilerParams(
             collective_id=0, has_side_effects=True, vmem_limit_bytes=56 * 1024 * 1024
         ),
     )(
-        ssm_input, gate_input, write_proj, read_proj, decay_codes, decay_rate[:, None],
-        jnp.repeat(skip_gain, HEAD_DIM)[None, :], norm_gain[None, :],
+        ssm_input, gate_input, write_proj, read_proj, decay_codes, decay_rate[None, :],
+        skip_gain[None, :],
     )
+    tile = GROUP // 2
+    return pl.pallas_call(
+        apply_norm,
+        grid=(rows // tile,),
+        out_shape=jax.ShapeDtypeStruct((rows, width), jnp.bfloat16),
+        in_specs=[
+            pl.BlockSpec((tile, width), lambda i: (i, 0)),
+            pl.BlockSpec((tile, HEAD_DIM), lambda i: (i, 0)),
+            pl.BlockSpec((1, width), lambda i: (0, 0)),
+        ],
+        out_specs=pl.BlockSpec((tile, width), lambda i: (i, 0)),
+        compiler_params=pltpu.CompilerParams(vmem_limit_bytes=56 * 1024 * 1024),
+    )(gated, scale, norm_gain[None, :])
 
 
 def solution(mesh):

time: 56.9 us -> 52.6 us (0.924)
  local copies, waits for them, and re-layouts: 7.44 us -> 0 us
  Pallas kernels: 49.3 us -> 52.3 us
    unnamed x1 -> x0, local copies, waits for them, and re-layouts: 4.79 us -> none
    pallas_call x1 -> x2, Pallas kernels: 49.3 us -> 52.3 us  [the longest x1 45.2 us: local(): pl.pallas_call(functools.partial(kernel, sections, groups), out_shape=(ja...]
    broadcast_in_dim x2 -> x0, local copies, waits for them, and re-layouts: 2.65 us -> none  [the longest x1 1.33 us: local(): decay_rate[:, None]]
where the time goes in v2:
time: 52.6 us; the launch traced here: 52.3 us
  Pallas kernels  52.3 us (99%)
    pallas_call x1, Pallas kernels, local(): pl.pallas_call(functools.partial(kernel, sections, groups), out_shape=(ja...  45.2 us
    pallas_call x1, Pallas kernels, local(): pl.pallas_call(apply_norm, grid=(rows // tile,), out_shape=jax.ShapeDtype...  7.12 us

profile of v2, /device:TPU:27, one launch (start us, length us, event | category | flops | bytes accessed | tf_op | source)
XLA Modules:
  0.0 52.3 jit_solution(9566349720890210655)
XLA Ops:
  0.0 45.2 %shard_map.82 = (bf16[1024,2048]{1,0:T(8,128)(2,1)}, f32[1024,128]{1,0:T(8,128)}) custom-call(bf16[1024,2048]{1,0:T(8,128)(2,1)} %x_hbm.1, bf16[1024,2048]{1,0:T(8,128)(2,1)} %g_hbm.1, bf16[1024,128]{1,0:T(8,128)(2,1)} %b_ref.1, bf16[1024,128]{1,0:T(8,128)(2,1)} %c_ref.1, s32[16,1024]{1,0:T(8,128)} %codes_ref.1, f32[1,16]{1,0:T(1,128)} %bitcast.4, ...), custom_call_target="tpu_custom_call" | custom-call | tf_op jit(solution)/shard_map/pallas_call | solution.py:314
  45.2 7.1 %shard_map.83 = bf16[1024,2048]{1,0:T(8,128)(2,1)} custom-call(bf16[1024,2048]{1,0:T(8,128)(2,1)} %get-tuple-element.7.gated_ref, f32[1024,128]{1,0:T(8,128)} %get-tuple-element.8.scale_ref, f32[1,2048]{1,0:T(1,128)} %bitcast.3), custom_call_target="tpu_custom_call" | custom-call | tf_op jit(solution)/shard_map/pallas_call | solution.py:366

commit v3 on v2

--- a/solution.py
+++ b/solution.py
@@ -170,7 +170,7 @@
         return carry
 
     units = blocks * TEAM
-    before = jnp.minimum(6 + 3 * z, units)
+    before = jnp.minimum(6 + 2 * z, units)
     lax.fori_loop(0, before, inner, 0)
 
     for i in range(1, TEAM):
@@ -289,14 +289,6 @@
     lax.fori_loop(0, blocks, norm, 0)
     for p in range(TEAM):
         put(p).wait()
-
-
-def apply_norm(gated_ref, scale_ref, gain_ref, out_ref):
-    scale = scale_ref[...]
-    for at in range(0, gated_ref.shape[1], HEAD_DIM):
-        own = slice(at, at + HEAD_DIM)
-        value = gated_ref[:, own].astype(F32) * scale * gain_ref[:, own]
-        out_ref[:, own] = value.astype(jnp.bfloat16)
 
 
 def local(
@@ -362,19 +354,8 @@
         ssm_input, gate_input, write_proj, read_proj, decay_codes, decay_rate[None, :],
         skip_gain[None, :],
     )
-    tile = GROUP // 2
-    return pl.pallas_call(
-        apply_norm,
-        grid=(rows // tile,),
-        out_shape=jax.ShapeDtypeStruct((rows, width), jnp.bfloat16),
-        in_specs=[
-            pl.BlockSpec((tile, width), lambda i: (i, 0)),
-            pl.BlockSpec((tile, HEAD_DIM), lambda i: (i, 0)),
-            pl.BlockSpec((1, width), lambda i: (0, 0)),
-        ],
-        out_specs=pl.BlockSpec((tile, width), lambda i: (i, 0)),
-        compiler_params=pltpu.CompilerParams(vmem_limit_bytes=56 * 1024 * 1024),
-    )(gated, scale, norm_gain[None, :])
+    value = gated.astype(F32) * scale[:, :1] * norm_gain[None, :]
+    return value.astype(jnp.bfloat16)
 
 
 def solution(mesh):

time: 52.6 us -> 51.9 us (0.987)
  Pallas kernels: 52.3 us -> 45.2 us
  other arithmetic: 0 us -> 5.22 us
  local copies, waits for them, and re-layouts: 0 us -> 1.25 us
    pallas_call x1 -> x0, Pallas kernels: 7.12 us -> none  [local(): pl.pallas_call(apply_norm, grid=(rows // tile,), out_shape=jax.ShapeDtype...]
    convert_element_type x0 -> x1, other arithmetic: none -> 5.22 us  [local(): return value.astype(jnp.bfloat16)]
    slice x0 -> x1, local copies, waits for them, and re-layouts: none -> 1.25 us  [local(): value = gated.astype(F32) * scale[:, :1] * norm_gain[None, :]]
where the time goes in v3:
time: 51.9 us; the launch traced here: 51.7 us
  Pallas kernels  45.2 us (87%)
  other arithmetic  5.22 us (10%)
  local copies, waits for them, and re-layouts  1.25 us (2%)
    pallas_call x1, Pallas kernels, local(): pl.pallas_call(functools.partial(kernel, sections, groups), out_shape=(ja...  45.2 us
    convert_element_type x1, other arithmetic, local(): return value.astype(jnp.bfloat16)  5.22 us
    slice x1, local copies, waits for them, and re-layouts, local(): value = gated.astype(F32) * scale[:, :1] * norm_gain[None, :]  1.25 us

profile of v3, /device:TPU:27, one launch (start us, length us, event | category | flops | bytes accessed | tf_op | source)
XLA Modules:
  0.0 51.7 jit_solution(13726775545075807005)
XLA Ops:
  0.0 0.0 copy-start
  0.0 45.2 %shard_map.82 = (bf16[1024,2048]{1,0:T(8,128)(2,1)}, f32[1024,128]{1,0:T(8,128)}) custom-call(bf16[1024,2048]{1,0:T(8,128)(2,1)} %x_hbm.1, bf16[1024,2048]{1,0:T(8,128)(2,1)} %g_hbm.1, bf16[1024,128]{1,0:T(8,128)(2,1)} %b_ref.1, bf16[1024,128]{1,0:T(8,128)(2,1)} %c_ref.1, s32[16,1024]{1,0:T(8,128)} %codes_ref.1, f32[1,16]{1,0:T(1,128)} %bitcast.2, ...), custom_call_target="tpu_custom_call" | custom-call | tf_op jit(solution)/shard_map/pallas_call | solution.py:306
  45.2 1.2 %slice_reduce_fusion = f32[1024]{0:T(1024)S(1)} fusion(f32[1024,128]{1,0:T(8,128)} %get-tuple-element.8), kind=kLoop, calls=%fused_computation.1 | loop fusion | bytes 8192 | tf_op jit(solution)/shard_map/slice | solution.py:357
  46.5 0.0 copy-done
  46.5 5.2 %multiply_convert_fusion = bf16[1024,2048]{1,0:T(8,128)(2,1)} fusion(bf16[1024,2048]{1,0:T(8,128)(2,1)} %get-tuple-element.7, f32[2048]{0:T(1024)S(1)} %copy-done, f32[1024]{0:T(1024)S(1)} %slice_reduce_fusion), kind=kLoop, calls=%fused_computation | loop fusion | flops 8388608 | bytes 8400896 | tf_op jit(solution)/shard_map/convert_element_type | solution.py:358
Async XLA Ops:
  0.0 46.5 %copy-start = (f32[2048]{0:T(1024)S(1)}, f32[2048]{0:T(1024)}, u32[]{:S(2)}) copy-start(f32[2048]{0:T(1024)} %param.15) | copy-start | bytes 24580
